TPU v7x, 128 devices: a whole 4x4x4 slice. The times are simulated.
128 devices in a mesh: seq: 8 (over x_lo, z), res: 16 (over x_hi, y, core).
Axes of the slice: x: 4 (x_hi: 2, x_lo: 2; x = x_hi * 2 + x_lo), y: 4, z: 4, core: 2. Of those that a mesh axis runs over, the one named last changes fastest.
Arguments:
- alignment_features: bfloat16 [96, 1024, 256], P('seq', 'res'), may hold values from -6 to 6
- couple_features: bfloat16 [1024, 1024, 128], P('res', 'seq'), may hold values from -8 to 8
- result_adjoint: bfloat16 [96, 1024, 256], P('seq', 'res'), may hold values from -6 to 6
- asking_projector: bfloat16 [256, 256], replicated, may hold values from -0.375 to 0.375
- lookup_projector: bfloat16 [256, 256], replicated, may hold values from -0.375 to 0.375
- content_projector: bfloat16 [256, 256], replicated, may hold values from -0.375 to 0.375
- sigmoid_projector: bfloat16 [256, 256], replicated, may hold values from -0.375 to 0.375
- final_projector: bfloat16 [256, 256], replicated, may hold values from -0.375 to 0.375
- couple_offset_projector: float32 [128, 8], replicated, may hold values from -8 to 8
- position_real_indicator: int32 [1024], replicated, may hold values from 0 to 1, as said below
- aligned_real_indicator: int32 [96], P('seq'), may hold values 0 or 1
Outputs:
- alignment_derivative: bfloat16 [96, 1024, 256], P('seq', 'res')
- couple_derivative: float32 [1024, 1024, 128], P('res', 'seq')
Inputs may be any that keep to these rules, and one draw needn't show every extreme that they name: `position_real_indicator`: the real residues are a leading run of at least 513 residues; the rest is padding.
All inputs are finite; a program needn't handle non-finite values. No bound on the sum of `aligned_real_indicator` on one device may be relied on, other than what follows from the above.
Results may differ from a plain program's by a relative error of at most 0.018.
Values may be sent and summed in bfloat16 or wider, within the bound.
A program may use at most 192 MiB of HBM per device.

v0:
```python
import jax
import jax.numpy as jnp
from jax import lax
from jax.sharding import PartitionSpec as P


def standardize_entries(values_in):
    row_mean = jnp.mean(values_in, -1, keepdims=True)
    centered = values_in - row_mean
    variance = jnp.mean(centered * centered, -1, keepdims=True)
    return centered * lax.rsqrt(variance + 1e-05)


def tile_bias(pair_tile, couple_offset_projector):
    return jnp.einsum(
        "ijc,ch->hij",
        standardize_entries(pair_tile),
        couple_offset_projector,
        precision=lax.Precision.HIGHEST,
    )


def body(
    alignment_features,
    couple_features,
    result_adjoint,
    asking_projector,
    lookup_projector,
    content_projector,
    sigmoid_projector,
    final_projector,
    couple_offset_projector,
    position_real_indicator,
    aligned_real_indicator,
):
    aligned_lines, position_lines, feature_depth = alignment_features.shape
    head_count = couple_offset_projector.shape[1]
    inner_width = asking_projector.shape[1]
    head_size = inner_width // head_count
    score_scale = head_size ** (-0.5)
    total_res = position_real_indicator.shape[0]
    alignment_real = alignment_features.astype(jnp.float32)
    standardized_couple = standardize_entries(alignment_real).astype(jnp.bfloat16)
    merged_lines = standardized_couple.reshape(-1, feature_depth)
    queries = (
        jnp.dot(merged_lines, asking_projector, preferred_element_type=jnp.float32) * score_scale
    ).astype(jnp.bfloat16)
    queries = queries.reshape(aligned_lines, position_lines, head_count, head_size)
    gate_act = jax.nn.sigmoid(
        jnp.dot(merged_lines, sigmoid_projector, preferred_element_type=jnp.float32)
    )
    gate_act = gate_act.reshape(aligned_lines, position_lines, inner_width)
    w_pair = jnp.concatenate([lookup_projector, content_projector], 1)
    pair_float = couple_features.astype(jnp.float32)
    tile_terms = tile_bias(pair_float, couple_offset_projector)
    bias_rows = lax.all_gather(tile_terms, "seq", axis=2, tiled=True)
    key_value = jnp.einsum(
        "yiw,wk->yik",
        lax.all_gather(standardized_couple, "res", axis=1, tiled=True),
        w_pair,
        preferred_element_type=jnp.float32,
    ).astype(jnp.bfloat16)
    usable = position_real_indicator > 0
    keep_rows = aligned_real_indicator.astype(jnp.bfloat16)

    def alone_aligned_entry(offset_derivative, bundled_operands):
        q_row, gate_row, pair_row, line_derivative, line_retain_indicator = bundled_operands
        k_heads = pair_row[:, :inner_width].reshape(total_res, head_count, head_size)
        v_heads = pair_row[:, inner_width:].reshape(total_res, head_count, head_size)
        logits = (
            jnp.einsum("ihd,jhd->hij", q_row, k_heads, preferred_element_type=jnp.float32)
            + bias_rows
        )
        logits = jnp.where(usable[None, None, :], logits, -1000000000.0)
        attn_probs = jax.nn.softmax(logits, axis=-1)
        prob_half = attn_probs.astype(jnp.bfloat16)
        attended = jnp.einsum(
            "hij,jhd->ihd", prob_half, v_heads, preferred_element_type=jnp.float32
        )
        attended = attended.reshape(position_lines, inner_width)
        grad_in = line_derivative * line_retain_indicator
        d_gated = jnp.dot(grad_in, final_projector.T, preferred_element_type=jnp.float32)
        d_attended = (
            (d_gated * gate_row).astype(jnp.bfloat16).reshape(position_lines, head_count, head_size)
        )
        d_gate = (d_gated * attended * gate_row * (1.0 - gate_row)).astype(jnp.bfloat16)
        d_probs = jnp.einsum(
            "ihd,jhd->hij", d_attended, v_heads, preferred_element_type=jnp.float32
        )
        d_values = jnp.einsum(
            "hij,ihd->jhd", prob_half, d_attended, preferred_element_type=jnp.float32
        )
        d_logits = attn_probs * (d_probs - jnp.sum(attn_probs * d_probs, -1, keepdims=True))
        dlog_half = d_logits.astype(jnp.bfloat16)
        d_queries = score_scale * jnp.einsum(
            "hij,jhd->ihd", dlog_half, k_heads, preferred_element_type=jnp.float32
        )
        d_queries = d_queries.astype(jnp.bfloat16).reshape(position_lines, inner_width)
        d_keys = jnp.einsum("hij,ihd->jhd", dlog_half, q_row, preferred_element_type=jnp.float32)
        d_near = jnp.dot(d_queries, asking_projector.T, preferred_element_type=jnp.float32)
        d_near = d_near + jnp.dot(d_gate, sigmoid_projector.T, preferred_element_type=jnp.float32)
        d_far = jnp.concatenate(
            [d_keys.reshape(total_res, inner_width), d_values.reshape(total_res, inner_width)], 1
        )
        return (offset_derivative + d_logits, (d_near, d_far))

    start_bias = jnp.zeros((head_count, position_lines, total_res), jnp.float32)
    offset_derivative, (d_near, d_far) = lax.scan(
        alone_aligned_entry, start_bias, (queries, gate_act, key_value, result_adjoint, keep_rows)
    )
    w_back = w_pair.astype(jnp.float32).T
    d_key_part = (
        lax.psum_scatter(
            jnp.einsum("sre,ec->rsc", d_far, w_back, precision=lax.Precision.HIGHEST).astype(
                jnp.bfloat16
            ),
            "res",
            scatter_dimension=0,
            tiled=True,
        )
        .astype(jnp.float32)
        .transpose(1, 0, 2)
    )
    standardized_derivative = d_near + d_key_part
    discarded_result, adjoint_mapping = jax.vjp(standardize_entries, alignment_real)
    alignment_derivative = adjoint_mapping(standardized_derivative)[0].astype(jnp.bfloat16)
    d_tile = lax.psum_scatter(
        offset_derivative.astype(jnp.bfloat16), "seq", scatter_dimension=2, tiled=True
    ).astype(jnp.float32)
    discarded_result, pull_pair = jax.vjp(
        lambda tile_in: tile_bias(tile_in, couple_offset_projector), pair_float
    )
    couple_derivative = pull_pair(d_tile)[0]
    return (alignment_derivative, couple_derivative)


def solution(mesh):
    return jax.shard_map(
        body,
        mesh=mesh,
        in_specs=(
            P("seq", "res", None),
            P("res", "seq", None),
            P("seq", "res", None),
            P(),
            P(),
            P(),
            P(),
            P(),
            P(),
            P(),
            P("seq"),
        ),
        out_specs=(P("seq", "res", None), P("res", "seq", None)),
        check_vma=False,
    )
```

profile of v0, /device:TPU:1, one launch (start us, length us, event | category | flops | bytes accessed | tf_op | source)
XLA Modules:
  0.0 585.6 jit_solution(12811674904938280151)
XLA Ops:
  7.2 3.2 copy.40
  12.5 3.3 fusion.45
  21.8 38.6 %all-gather.5.cloned.1.call-done = f32[8,64,1024]{2,0,1:T(8,128)} async-done(((f32[8,64,128]{2,0,1:T(8,128)}), f32[8,64,1024]{2,0,1:T(8,128)}) %all-gather.5.cloned.1.call-update) | async-done | bytes 2097168 | tf_op jit(solution)/shard_map/all_gather | solution.py:56
  60.5 4.2 copy.44
  64.6 68.6 %all-gather.3.cloned.1.call-done = bf16[12,1024,256]{2,1,0:T(8,128)(2,1)} async-done(((bf16[12,64,256]{2,1,0:T(8,128)(2,1)}), bf16[12,1024,256]{2,1,0:T(8,128)(2,1)}) %all-gather.3.cloned.1.call-update) | async-done | bytes 6291472 | tf_op jit(solution)/shard_map/all_gather | solution.py:59
  133.3 9.2 %convolution_convert_fusion = bf16[12,1024,512]{2,1,0:T(8,128)(2,1)} fusion(bf16[12,1024,256]{2,1,0:T(8,128)(2,1)} %all-gather.3.cloned.1.call-done, bf16[256,256]{1,0:T(8,128)(2,1)S(1)} %copy-done.23, bf16[256,256]{1,0:T(8,128)(2,1)S(1)} %copy-done.25), kind=kOutput, calls=%fused_computation.42 | convolution fusion | flops 3228041216 | bytes 19136512 | tf_op jit(solution)/shard_map/yiw,wk->yik/dot_general | solution.py:57
  142.5 296.8 %while.15 = (s32[]{:T(128)}, f32[8,64,1024]{2,1,0:T(8,128)}, f32[12,64,256]{2,1,0:T(8,128)}, f32[12,1024,512]{1,2,0:T(8,128)}, pred[1024]{0:T(1024)(128)(4,1)S(1...) while((s32[]{:T(128)}, f32[8,64,1024]{2,1,0:T(8,128)}, ...), condition=%wide.region_8.9_spmd.clone, body=%wide.region_4.8_spmd.clone.sunk | while | flops 237161984 | bytes 90401080 | solution.py:108
  143.2 2.2 fusion.141
  154.3 2.9 fusion.147
  158.2 2.4 multiply_reduce_fusion.2
  162.5 2.1 fusion.146
  168.0 2.2 fusion.141
  179.0 2.9 fusion.147
  182.9 2.4 multiply_reduce_fusion.2
  187.2 2.1 fusion.146
  192.7 2.2 fusion.141
  203.8 2.9 fusion.147
  207.7 2.4 multiply_reduce_fusion.2
  211.9 2.1 fusion.146
  217.5 2.2 fusion.141
  228.5 2.9 fusion.147
  232.4 2.4 multiply_reduce_fusion.2
  236.7 2.1 fusion.146
  242.2 2.2 fusion.141
  253.3 2.9 fusion.147
  257.2 2.4 multiply_reduce_fusion.2
  261.4 2.1 fusion.146
  267.0 2.2 fusion.141
  278.0 2.9 fusion.147
  281.9 2.4 multiply_reduce_fusion.2
  286.2 2.1 fusion.146
  291.7 2.2 fusion.141
  302.7 2.9 fusion.147
  306.6 2.4 multiply_reduce_fusion.2
  310.9 2.1 fusion.146
  316.4 2.2 fusion.141
  327.5 2.9 fusion.147
  331.4 2.4 multiply_reduce_fusion.2
  335.7 2.1 fusion.146
  341.1 2.2 fusion.141
  352.2 2.9 fusion.147
  356.1 2.4 multiply_reduce_fusion.2
  360.4 2.1 fusion.146
  365.9 2.2 fusion.141
  376.9 2.9 fusion.147
  380.8 2.4 multiply_reduce_fusion.2
  385.1 2.1 fusion.146
  390.6 2.2 fusion.141
  401.6 2.9 fusion.147
  405.5 2.4 multiply_reduce_fusion.2
  409.8 2.1 fusion.146
  415.3 2.2 fusion.141
  426.4 2.9 fusion.147
  430.3 2.4 multiply_reduce_fusion.2
  434.6 2.1 fusion.146
  439.3 2.8 convert_element_type.60
  442.2 2.6 copy.54
  444.8 2.1 reshape.101
  447.2 26.2 %convert_bitcast_fusion = bf16[1024,12,256]{2,0,1:T(8,128)(2,1)} fusion(f32[12,1024,512]{1,2,0:T(8,128)} %get-tuple-element.415, bf16[256,256]{1,0:T(8,128)(2,1)S(1)} %copy-done.24, bf16[256,256]{1,0:T(8,128)(2,1)S(1)} %copy-done.26), kind=kOutput, calls=%fused_computation.44 | convolution fusion | flops 19331022848 | bytes 31719424 | tf_op jit(solution)/shard_map/sre,ec->rsc/dot_general | solution.py:114
  473.4 5.5 reduce-scatter.7.cloned.1.call-done
  480.2 2.3 fusion.37
  484.2 3.3 broadcast_add_fusion
  487.5 5.7 copy.48
  493.1 81.7 %reduce-scatter.5.cloned.1.call-done = bf16[64,12,256]{2,0,1:T(8,128)(2,1)} async-done(((bf16[1024,12,256]{2,0,1:T(8,128)(2,1)}), bf16[64,12,256]{2,0,1:T(8,128)(2,1)}) %reduce-scatter.5.cloned.1.call-update) | async-done | bytes 393232 | tf_op jit(solution)/shard_map/reduce_scatter | solution.py:113
  (616 shorter events, 194.8 us)
Async XLA Ops:
  7.2 5.3 copy-start
  7.2 53.3 %all-gather.5.cloned.1.call-start = ((), (), s32[]{:S(2)}) async-start(), calls=%async_computation.3 | async-start | bytes 2359296 | tf_op jit(solution)/shard_map/all_gather | solution.py:56
  11.0 4.8 copy-start.19
  12.5 5.0 copy-start.29
  12.5 5.3 copy-start.38
  12.5 5.3 copy-start.11
  15.9 117.4 %all-gather.3.cloned.1.call-start = ((), (), s32[]{:S(2)}) async-start(), calls=%async_computation.2 | async-start | bytes 6684672 | tf_op jit(solution)/shard_map/all_gather | solution.py:59
  17.5 461.3 %reduce-scatter.7.cloned.1.call-start = ((), (), s32[]{:S(2)}) async-start(), calls=%async_computation.5 | async-start | bytes 1179648
  21.8 111.5 %copy-start.23 = (bf16[256,256]{1,0:T(8,128)(2,1)S(1)}, bf16[256,256]{1,0:T(8,128)(2,1)}, u32[]{:S(2)}) copy-start(bf16[256,256]{1,0:T(8,128)(2,1)} %param.18) | copy-start | bytes 393220
  21.8 111.5 %copy-start.25 = (bf16[256,256]{1,0:T(8,128)(2,1)S(1)}, bf16[256,256]{1,0:T(8,128)(2,1)}, u32[]{:S(2)}) copy-start(bf16[256,256]{1,0:T(8,128)(2,1)} %param.17) | copy-start | bytes 393220
  64.6 77.9 %copy-start.15 = (bf16[256,256]{1,0:T(8,128)(2,1)S(1)}, bf16[256,256]{1,0:T(8,128)(2,1)}, u32[]{:S(2)}) copy-start(bf16[256,256]{1,0:T(8,128)(2,1)} %param.20) | copy-start | bytes 393220
  142.5 5.5 copy-start.39
  142.5 5.6 copy-start.35
  161.8 3.9 copy-start.6
  161.8 3.9 copy-start.7
  167.3 5.5 copy-start.39
  167.3 5.6 copy-start.35
  186.6 3.9 copy-start.6
  186.6 3.9 copy-start.7
  192.0 5.5 copy-start.39
  192.0 5.6 copy-start.35
  211.3 3.9 copy-start.6
  211.3 3.9 copy-start.7
  216.7 5.5 copy-start.39
  216.7 5.6 copy-start.35
  236.0 3.9 copy-start.6
  236.1 3.9 copy-start.7
  241.5 5.5 copy-start.39
  241.5 5.6 copy-start.35
  260.8 3.9 copy-start.6
  260.8 3.9 copy-start.7
  266.3 5.5 copy-start.39
  266.3 5.6 copy-start.35
  285.6 3.9 copy-start.6
  291.0 5.5 copy-start.39
  291.0 5.6 copy-start.35
  310.3 3.9 copy-start.6
  310.3 3.9 copy-start.7
  315.7 5.5 copy-start.39
  315.7 5.6 copy-start.35
  335.0 3.9 copy-start.6
  335.0 3.9 copy-start.7
  340.4 5.5 copy-start.39
  340.4 5.6 copy-start.35
  359.7 3.9 copy-start.6
  359.7 3.9 copy-start.7
  365.1 5.5 copy-start.39
  365.2 5.6 copy-start.35
  384.4 3.9 copy-start.6
  384.5 3.9 copy-start.7
  389.9 5.5 copy-start.39
  389.9 5.6 copy-start.35
  409.2 3.9 copy-start.6
  409.2 3.9 copy-start.7
  414.6 5.5 copy-start.39
  414.6 5.6 copy-start.35
  433.9 3.9 copy-start.6
  433.9 3.9 copy-start.7
  446.9 127.9 %reduce-scatter.5.cloned.1.call-start = ((), (), s32[]{:S(2)}) async-start(), calls=%async_computation.4 | async-start | bytes 6684672 | tf_op jit(solution)/shard_map/reduce_scatter | solution.py:113
  473.4 6.8 %copy-start.4 = (bf16[64,128,128]{1,2,0:T(8,128)(2,1)S(1)}, bf16[64,128,128]{1,2,0:T(8,128)(2,1)}, u32[]{:S(2)}) copy-start(bf16[64,128,128]{1,2,0:T(8,128)(2,1)} %copy-done.3) | copy-start | bytes 6291460
  473.4 6.8 %copy-start.20 = (f32[64,128]{1,0:T(8,128)S(1)}, f32[64,128]{1,0:T(8,128)}, u32[]{:S(2)}) copy-start(f32[64,128]{1,0:T(8,128)} %copy-done.19) | copy-start | bytes 98308
  487.5 87.4 %copy-start.9 = (f32[12,64,256]{2,1,0:T(8,128)S(1)}, f32[12,64,256]{2,1,0:T(8,128)}, u32[]{:S(2)}) copy-start(f32[12,64,256]{2,1,0:T(8,128)} %get-tuple-element.414) | copy-start | bytes 2359300
  487.5 88.8 %copy-start.34 = (f32[12,64]{1,0:T(8,128)S(1)}, f32[12,64]{1,0:T(8,128)}, u32[]{:S(2)}) copy-start(f32[12,64]{1,0:T(8,128)} %copy-done.33) | copy-start | bytes 9220
  487.5 88.8 %copy-start.32 = (f32[12,64]{1,0:T(8,128)S(1)}, f32[12,64]{1,0:T(8,128)}, u32[]{:S(2)}) copy-start(f32[12,64]{1,0:T(8,128)} %copy-done.31) | copy-start | bytes 9220
  (146 other events, 278.6 us)
Sparse Core Ops, SparseCore 0:
  16.0 44.4 all-gather.4
  63.6 69.6 all-gather.2
  447.0 31.7 reduce-scatter.6
  482.9 91.8 reduce-scatter.4
where the time goes:
time: 591 us; the launch traced here: 586 us
  matrix products  213 us (36%)
  waiting for transfers between devices  194 us (33%)
  local copies, waits for them, and re-layouts  98.5 us (17%)
  other arithmetic  62 us (10%)
  between operations  14.2 us (2%)
    reduce_scatter x1, waiting for transfers between devices, body(): lax.psum_scatter(jnp.einsum('sre,ec->rsc', d_far, w_back, precision=lax.P...  81.7 us
    all_gather x1, waiting for transfers between devices, body(): lax.all_gather(standardized_couple, 'res', axis=1, tiled=True)  68.6 us
    all_gather x1, waiting for transfers between devices, body(): bias_rows = lax.all_gather(tile_terms, 'seq', axis=2, tiled=True)  38.6 us
    dot_general x12, matrix products, alone_aligned_entry(): jnp.einsum('hij,ihd->jhd', prob_half, d_attended, preferred_element_type=...  34.7 us
    dynamic_slice x36, local copies, waits for them, and re-layouts, body(): lax.scan(alone_aligned_entry, start_bias, (queries, gate_act, key_value,...  30.2 us
    dot_general x12, matrix products, alone_aligned_entry(): jnp.einsum('ihd,jhd->hij', d_attended, v_heads, preferred_element_type=jn...  28.3 us
    dot_general x12, matrix products, alone_aligned_entry(): jnp.dot(grad_in, final_projector.T, preferred_element_type=jnp.float32)  26.5 us
    dot_general x1, matrix products, body(): jnp.einsum('sre,ec->rsc', d_far, w_back, precision=lax.Precision.HIGHEST)  26.2 us
  transfers between devices with their start and end apart: 4, of which 4 were waited for; matrix products, arithmetic and copies ran while one was open for 9% of the time, Pallas kernels for 0%

commit v1 on v0

v1 whole, which is shorter than its diff:
```python
import jax
import jax.numpy as jnp
from jax import lax
from jax.experimental import pallas as pl
from jax.experimental.pallas import tpu as pltpu
from jax.sharding import PartitionSpec as P

BF = jnp.bfloat16
F32 = jnp.float32
MESH = pl.DeviceIdType.MESH
EPS = 1e-05

SEQS = 6
ROWS = 128
HALF = 64
RES = 1024
WIDTH = 256
HEADS = 8
HD = 32
PEERS = 8
CH = 2
NCH = HEADS // CH

NN = (((1,), (0,)), ((), ()))
NT = (((1,), (1,)), ((), ()))
TT = (((0,), (1,)), ((), ()))


def dot(a, b, dims=NN):
    return lax.dot_general(a, b, dims, preferred_element_type=F32)


def layer_norm_parts(x):
    mean = jnp.mean(x, -1, keepdims=True)
    cen = x - mean
    var = jnp.mean(cen * cen, -1, keepdims=True)
    rstd = lax.rsqrt(var + EPS)
    return cen * rstd, rstd


def split(x):
    hi = x.astype(BF)
    return hi, (x - hi.astype(F32)).astype(BF)


def main_kernel(
    x_ref, pair_ref, g_ref, wq, wk, wv, wg, wo, wp_ref, mask_ref, keep_ref,
    out_ref, dtile_ref,
    xraw, graw, xg, bias, dbias, btmp, kt, vt, q_s, do_s, doT, qT, o_s, dq_s, dkt, dvt,
    dnear, dfar, rsbuf, ostage, orecv, dxs, dxr, dbs, dbr,
    sx_s, sx_r, ag_s, ag_r, rs_s, rs_r, bi_s, bi_r, bf_s, bf_r, dx_s, dx_r, ds_s, ds_r, oo_s, oo_r,
):
    sq = lax.axis_index("seq")
    rs = lax.axis_index("res")
    p = lax.rem(rs, 2)
    c = lax.div(rs, 2)
    other = 1 - p
    partner = (sq, rs + 1 - 2 * p)

    def res_peer(d):
        return (sq, lax.rem(c + d, PEERS) * 2 + p)

    def seq_peer(d):
        return (lax.rem(sq + d, PEERS), rs)

    bar = pltpu.get_barrier_semaphore()
    pl.semaphore_signal(bar, inc=1, device_id=partner, device_id_type=MESH)
    for d in range(1, PEERS):
        pl.semaphore_signal(bar, inc=1, device_id=res_peer(d), device_id_type=MESH)
        pl.semaphore_signal(bar, inc=1, device_id=seq_peer(d), device_id_type=MESH)
    pl.semaphore_wait(bar, 2 * PEERS - 1)

    my_rows = pl.ds(pl.multiple_of(p * HALF, HALF), HALF)
    other_rows = pl.ds(pl.multiple_of(other * HALF, HALF), HALF)
    chip_rows = pl.ds(pl.multiple_of(c * ROWS, ROWS), ROWS)
    my_cols = pl.ds(pl.multiple_of(sq * ROWS, ROWS), ROWS)

    def swap_copy(i, src, dst):
        return pltpu.make_async_remote_copy(
            src.at[pl.ds(other * SEQS, SEQS)], dst.at[:, my_rows, :], sx_s.at[i], sx_r.at[i],
            device_id=partner, device_id_type=MESH,
        )

    swaps = [swap_copy(0, x_ref, xraw), swap_copy(1, g_ref, graw)]
    for cp in swaps:
        cp.start()
    xraw[:, my_rows, :] = x_ref[pl.ds(p * SEQS, SEQS)]
    graw[:, my_rows, :] = g_ref[pl.ds(p * SEQS, SEQS)]

    def gather_copy(s, d):
        blk = xg.at[s, chip_rows, :]
        return pltpu.make_async_remote_copy(
            blk, blk, ag_s.at[s, d], ag_r.at[s, d], device_id=res_peer(d), device_id_type=MESH
        )

    for cp in swaps:
        cp.wait_recv()

    def norm_body(s, carry):
        xhat, rstd = layer_norm_parts(xraw[s].astype(F32))
        xg[s, chip_rows, :] = xhat.astype(BF)
        for d in range(1, PEERS):
            gather_copy(s, d).start()
        return carry

    lax.fori_loop(0, SEQS, norm_body, 0)

    w_hi, w_lo = split(wp_ref[...].T)
    left = jnp.concatenate(
        [jnp.concatenate([w_hi, w_hi], 1), jnp.concatenate([w_lo, jnp.zeros_like(w_lo)], 1)], 0
    )
    ones = jnp.ones((8, WIDTH), BF)

    def pair_body(i, carry):
        x = pair_ref[i].astype(F32)
        cen = x - jnp.mean(x, -1, keepdims=True)
        c_hi, c_lo = split(cen)
        s_hi, s_lo = split(cen * cen)
        y = dot(left, jnp.concatenate([c_hi, c_lo], 1), NT)
        var = dot(ones, jnp.concatenate([s_hi, s_lo], 1), NT) * (1.0 / 128)
        btmp[pl.ds(pl.multiple_of(i * 8, 8), 8), :] = (y[0:8] + y[8:16]) * lax.rsqrt(var + EPS)
        return carry

    lax.fori_loop(0, HALF, pair_body, 0, unroll=8)

    def bias_copy(k, d):
        blk = bias.at[pl.ds(k * CH, CH), my_rows, my_cols]
        return pltpu.make_async_remote_copy(
            blk, blk, bi_s.at[k, d], bi_r.at[k, d], device_id=seq_peer(d), device_id_type=MESH
        )

    def forward_copy(k):
        blk = bias.at[pl.ds(k * CH, CH), my_rows, :]
        return pltpu.make_async_remote_copy(
            blk, blk, bf_s.at[k], bf_r.at[k], device_id=partner, device_id_type=MESH
        )

    usable = mask_ref[pl.ds(sq, 1), :] > 0
    for k in range(NCH):
        for h in range(k * CH, k * CH + CH):
            bias[h, my_rows, my_cols] = jnp.where(
                usable, btmp[pl.ds(h, HALF, stride=8), :], -1000000000.0
            )
        for d in range(1, PEERS):
            bias_copy(k, d).start()

    def bias_arrive(k):
        for d in range(1, PEERS):
            bias_copy(k, d).wait_recv()
        forward_copy(k).start()

    def scatter_copy(s, d):
        cols = pl.ds(pl.multiple_of(lax.rem(c + d, PEERS) * ROWS, ROWS), ROWS)
        return pltpu.make_async_remote_copy(
            dfar.at[s, :, cols], rsbuf.at[s, d], rs_s.at[s, d], rs_r.at[s, d],
            device_id=res_peer(d), device_id_type=MESH,
        )

    dbias[...] = jnp.zeros_like(dbias)
    scale = HD ** (-0.5)

    def finish_seq(s):
        for d in range(1, PEERS):
            scatter_copy(s, d).wait_recv()
        far = dfar[s, :, chip_rows].astype(F32)
        for d in range(1, PEERS):
            far = far + rsbuf[s, d].astype(F32)
        dn = dnear[s] + far.T
        xhat, rstd = layer_norm_parts(xraw[s].astype(F32))
        dx = rstd * (
            dn
            - jnp.mean(dn, -1, keepdims=True)
            - xhat * jnp.mean(dn * xhat, -1, keepdims=True)
        )
        ostage[s] = dx.astype(BF)

    def seq_body(s, carry):
        for d in range(1, PEERS):
            gather_copy(s, d).wait_recv()
        x = xg[s]
        kt[...] = dot(wk[...], x, TT).astype(BF)
        vt[...] = dot(wv[...], x, TT).astype(BF)
        xq = xg[s, chip_rows, :]
        qf = dot(xq, wq[...]) * scale
        q_s[...] = qf.astype(BF)
        qT[...] = qf.T.astype(BF)
        gate = jax.nn.sigmoid(dot(xq, wg[...]))
        keep = keep_ref[p * SEQS + s].astype(F32)
        grad_in = (graw[s].astype(F32) * keep).astype(BF)
        dg = dot(grad_in, wo[...], NT)
        d_att = dg * gate
        do_s[...] = d_att.astype(BF)
        doT[...] = d_att.T.astype(BF)

        @pl.when(s == 0)
        def _():
            bias_arrive(0)

        for h in range(HEADS):
            hs = slice(HD * h, HD * h + HD)
            if h % CH == 0:
                k = h // CH

                @pl.when(s == 0)
                def _():
                    if k + 1 < NCH:
                        bias_arrive(k + 1)
                    forward_copy(k).wait_recv()

            logits = dot(q_s[:, hs], kt[hs, :]) + bias[h]
            top = jnp.max(logits, -1, keepdims=True)
            e = jnp.exp(logits - top)
            prob = e * (1.0 / jnp.sum(e, -1, keepdims=True))
            prob_half = prob.astype(BF)
            d_prob = dot(do_s[:, hs], vt[hs, :])
            att = dot(prob_half, vt[hs, :], NT)
            o_s[:, hs] = att
            inner = jnp.sum(att * do_s[:, hs].astype(F32), -1, keepdims=True)
            d_log = prob * (d_prob - inner)
            dbias[h] += d_log
            dlog_half = d_log.astype(BF)
            dq_s[:, hs] = (dot(dlog_half, kt[hs, :], NT) * scale).astype(BF)
            dvt[hs, :] = dot(doT[hs, :], prob_half).astype(BF)
            dkt[hs, :] = dot(qT[hs, :], dlog_half).astype(BF)

        d_gate = (dg * o_s[...] * gate * (1.0 - gate)).astype(BF)
        dnear[s] = dot(dq_s[...], wq[...], NT) + dot(d_gate, wg[...], NT)
        dfar[s] = (dot(wk[...], dkt[...]) + dot(wv[...], dvt[...])).astype(BF)
        for d in range(1, PEERS):
            scatter_copy(s, d).start()

        @pl.when(s >= 2)
        def _():
            finish_seq(s - 2)

        return carry

    lax.fori_loop(0, SEQS, seq_body, 0)

    def pair_swap(k):
        blk = pl.ds(k * CH, CH)
        return pltpu.make_async_remote_copy(
            dxs.at[blk], dxr.at[blk], dx_s.at[k], dx_r.at[k], device_id=partner, device_id_type=MESH
        )

    def tile_copy(k, d):
        cols = pl.ds(pl.multiple_of(lax.rem(sq + d, PEERS) * ROWS, ROWS), ROWS)
        blk = pl.ds(k * CH, CH)
        return pltpu.make_async_remote_copy(
            dbs.at[blk, :, cols], dbr.at[d, blk], ds_s.at[k, d], ds_r.at[k, d],
            device_id=seq_peer(d), device_id_type=MESH,
        )

    for k in range(NCH):
        blk = pl.ds(k * CH, CH)
        dxs[blk] = dbias[blk, other_rows, :].astype(BF)
        pair_swap(k).start()
    for k in range(NCH):
        blk = pl.ds(k * CH, CH)
        pair_swap(k).wait_recv()
        dbs[blk] = (dbias[blk, my_rows, :] + dxr[blk].astype(F32)).astype(BF)
        for d in range(1, PEERS):
            tile_copy(k, d).start()

    finish_seq(SEQS - 2)
    finish_seq(SEQS - 1)
    back = pltpu.make_async_remote_copy(
        ostage.at[:, other_rows, :], orecv, oo_s, oo_r, device_id=partner, device_id_type=MESH
    )
    back.start()
    out_ref[pl.ds(p * SEQS, SEQS)] = ostage[:, my_rows, :]

    for k in range(NCH):
        blk = pl.ds(k * CH, CH)
        for d in range(1, PEERS):
            tile_copy(k, d).wait_recv()
        tile = dbs[blk, :, my_cols].astype(F32)
        for d in range(1, PEERS):
            tile = tile + dbr[d, blk].astype(F32)
        dtile_ref[blk] = tile

    back.wait_recv()
    out_ref[pl.ds(other * SEQS, SEQS)] = orecv[...]

    for cp in swaps:
        cp.wait_send()
    back.wait_send()

    def drain_seq(s, carry):
        for d in range(1, PEERS):
            gather_copy(s, d).wait_send()
            scatter_copy(s, d).wait_send()
        return carry

    lax.fori_loop(0, SEQS, drain_seq, 0)

    def drain_chunk(k, carry):
        forward_copy(k).wait_send()
        pair_swap(k).wait_send()
        for d in range(1, PEERS):
            bias_copy(k, d).wait_send()
            tile_copy(k, d).wait_send()
        return carry

    lax.fori_loop(0, NCH, drain_chunk, 0)


def run_main(x, pair, g, wq, wk, wv, wg, wo, wp, mask, keep):
    def vm(*shape, dt=BF):
        return pltpu.VMEM(shape, dt)

    dma = pltpu.SemaphoreType.DMA
    vmem = pl.BlockSpec(memory_space=pltpu.VMEM)
    smem = pl.BlockSpec(memory_space=pltpu.SMEM)
    return pl.pallas_call(
        main_kernel,
        out_shape=(
            jax.ShapeDtypeStruct(x.shape, BF),
            jax.ShapeDtypeStruct((HEADS, HALF, ROWS), F32),
        ),
        in_specs=[vmem] * 10 + [smem],
        out_specs=[vmem, vmem],
        scratch_shapes=[
            vm(SEQS, ROWS, WIDTH),
            vm(SEQS, ROWS, WIDTH),
            vm(SEQS, RES, WIDTH),
            vm(HEADS, ROWS, RES, dt=F32),
            vm(HEADS, ROWS, RES, dt=F32),
            vm(HALF * 8, ROWS, dt=F32),
            vm(WIDTH, RES),
            vm(WIDTH, RES),
            vm(ROWS, WIDTH),
            vm(ROWS, WIDTH),
            vm(WIDTH, ROWS),
            vm(WIDTH, ROWS),
            vm(ROWS, WIDTH, dt=F32),
            vm(ROWS, WIDTH),
            vm(WIDTH, RES),
            vm(WIDTH, RES),
            vm(SEQS, ROWS, WIDTH, dt=F32),
            vm(SEQS, WIDTH, RES),
            vm(SEQS, PEERS, WIDTH, ROWS),
            vm(SEQS, ROWS, WIDTH),
            vm(SEQS, HALF, WIDTH),
            vm(HEADS, HALF, RES),
            vm(HEADS, HALF, RES),
            vm(HEADS, HALF, RES),
            vm(PEERS, HEADS, HALF, ROWS),
            dma((2,)), dma((2,)),
            dma((SEQS, PEERS)), dma((SEQS, PEERS)),
            dma((SEQS, PEERS)), dma((SEQS, PEERS)),
            dma((NCH, PEERS)), dma((NCH, PEERS)),
            dma((NCH,)), dma((NCH,)),
            dma((NCH,)), dma((NCH,)),
            dma((NCH, PEERS)), dma((NCH, PEERS)),
            dma, dma,
        ],
        compiler_params=pltpu.CompilerParams(
            collective_id=0, has_side_effects=True, vmem_limit_bytes=56 * 2**20
        ),
        name="attention_backward",
    )(x, pair, g, wq, wk, wv, wg, wo, wp, mask, keep)


PB = 8


def pair_kernel(pair_ref, d_ref, wp_ref, out_ref):
    w_hi, w_lo = split(wp_ref[...].T)
    w2 = jnp.concatenate([w_hi, w_lo, w_hi, w_lo], 0)
    for i in range(PB):
        xhat, rstd = layer_norm_parts(pair_ref[i].astype(F32))
        d_hi, d_lo = split(d_ref[:, i, :])
        dn = lax.dot_general(
            jnp.concatenate([d_hi, d_hi, d_lo, d_lo], 0), w2, (((0,), (0,)), ((), ())),
            preferred_element_type=F32,
        )
        out_ref[i] = rstd * (
            dn
            - jnp.mean(dn, -1, keepdims=True)
            - xhat * jnp.mean(dn * xhat, -1, keepdims=True)
        )


def run_pair(pair, dtile, wp):
    n = pair.shape[0]
    return pl.pallas_call(
        pair_kernel,
        grid=(n // PB,),
        out_shape=jax.ShapeDtypeStruct(pair.shape, F32),
        in_specs=[
            pl.BlockSpec((PB, 128, 128), lambda i: (i, 0, 0)),
            pl.BlockSpec((HEADS, PB, 128), lambda i: (0, i, 0)),
            pl.BlockSpec((128, HEADS), lambda i: (0, 0)),
        ],
        out_specs=pl.BlockSpec((PB, 128, 128), lambda i: (i, 0, 0)),
        name="pair_gradient",
    )(pair, dtile, wp)


def body(x, pair, g, wq, wk, wv, wg, wo, wp, mask, keep):
    dx, dtile = run_main(x, pair, g, wq, wk, wv, wg, wo, wp, mask.reshape(8, 128), keep)
    return dx, run_pair(pair, dtile, wp)


def solution(mesh):
    return jax.shard_map(
        body,
        mesh=mesh,
        in_specs=(
            P("seq", "res", None),
            P("res", "seq", None),
            P("seq", "res", None),
            P(),
            P(),
            P(),
            P(),
            P(),
            P(),
            P(),
            P("seq"),
        ),
        out_specs=(P("seq", "res", None), P("res", "seq", None)),
        check_vma=False,
    )
```

time: 591 us -> 164 us (0.28)
  matrix products: 213 us -> 0 us
  waiting for transfers between devices: 194 us -> 0 us
  Pallas kernels: 0 us -> 160 us
  local copies, waits for them, and re-layouts: 98.5 us -> 2.17 us
  other arithmetic: 62 us -> 0 us
  between operations: 14.2 us -> 0.65 us
    dot_general x114 -> x0, matrix products: 213 us -> none  [the longest x12 34.7 us: alone_aligned_entry(): jnp.einsum('hij,ihd->jhd', prob_half, d_attended, preferred_element_type=...]
    pallas_call x0 -> x2, Pallas kernels: none -> 160 us  [the longest x1 144 us: run_main(): pl.pallas_call(main_kernel, out_shape=(jax.ShapeDtypeStruct(x.shape, BF),...]
    all_gather x2 -> x0, waiting for transfers between devices: 107 us -> none  [the longest x1 68.6 us: body(): lax.all_gather(standardized_couple, 'res', axis=1, tiled=True)]
    reduce_scatter x1 -> x0, waiting for transfers between devices: 81.7 us -> none  [body(): lax.psum_scatter(jnp.einsum('sre,ec->rsc', d_far, w_back, precision=lax.P...]
    dynamic_slice x36 -> x0, local copies, waits for them, and re-layouts: 30.2 us -> none  [body(): lax.scan(alone_aligned_entry, start_bias, (queries, gate_act, key_value,...]
    while x360 -> x0, local copies, waits for them, and re-layouts: 24.9 us -> none
    sub x12 -> x0, other arithmetic: 20.6 us -> none  [alone_aligned_entry(): attn_probs = jax.nn.softmax(logits, axis=-1)]
    unnamed x59 -> x4, local copies, waits for them, and re-layouts: 21.2 us -> 2.17 us
  transfers between devices with their start and end apart: 4 -> 0, of which waited for: 4 -> 0; matrix products, arithmetic and copies ran while one was open for 9% -> 0% of each run, Pallas kernels for 0% -> 0%
where the time goes in v1:
time: 164 us; the launch traced here: 163 us
  Pallas kernels  160 us (98%)
  local copies, waits for them, and re-layouts  2.17 us (1%)
    pallas_call x1, Pallas kernels, run_main(): pl.pallas_call(main_kernel, out_shape=(jax.ShapeDtypeStruct(x.shape, BF),...  144 us
    pallas_call x1, Pallas kernels, run_pair(): pl.pallas_call(pair_kernel, grid=(n // PB,), out_shape=jax.ShapeDtypeStru...  15.9 us

profile of v1, /device:TPU:1, one launch (start us, length us, event | category | flops | bytes accessed | tf_op | source)
XLA Modules:
  0.0 162.5 jit_solution(8133486781784867571)
XLA Ops:
  0.6 1.4 copy.13.wp_ref
  2.0 143.8 %attention_backward.1 = (bf16[12,64,256]{2,1,0:T(8,128)(2,1)}, f32[8,64,128]{2,1,0:T(8,128)}) custom-call(bf16[12,64,256]{2,1,0:T(8,128)(2,1)} %x_ref.1, bf16[64,128,128]{2,1,0:T(8,128)(2,1)} %pair_ref.3, bf16[12,64,256]{2,1,0:T(8,128)(2,1)} %g_ref.1, bf16[256,256]{1,0:T(8,128)(2,1)} %wq.1, bf16[256,256]{1,0:T(8,128)(2,1)} %wk.1, bf16[256,256]{1,0:T(8,128)(2,1)} %wv.1, ...), custom_call_target="tpu_custom_call" | custom-call | tf_op jit(solution)/shard_map/attention_backward/pallas_call | solution.py:315
  145.9 0.0 copy-start
  145.9 15.9 %pair_gradient.1 = f32[64,128,128]{2,1,0:T(8,128)} custom-call(bf16[64,128,128]{2,1,0:T(8,128)(2,1)} %pair_ref.3, f32[8,64,128]{2,1,0:T(8,128)} %get-tuple-element.5.d_ref, f32[128,8]{1,0:T(8,128)} %copy.13.wp_ref), custom_call_target="tpu_custom_call" | custom-call | tf_op jit(solution)/shard_map/pair_gradient/pallas_call | solution.py:387
  161.8 0.0 copy-done
  161.8 0.7 copy.16
Async XLA Ops:
  145.9 15.9 %copy-start = (bf16[12,64,256]{2,1,0:T(8,128)(2,1)S(1)}, bf16[12,64,256]{2,1,0:T(8,128)(2,1)}, u32[]{:S(2)}) copy-start(bf16[12,64,256]{2,1,0:T(8,128)(2,1)} %get-tuple-element.8) | copy-start | bytes 1179652

commit v2 on v1

v2 whole, which is shorter than its diff:
```python
import jax
import jax.numpy as jnp
from jax import lax
from jax.experimental import pallas as pl
from jax.experimental.pallas import tpu as pltpu
from jax.sharding import PartitionSpec as P

BF = jnp.bfloat16
F32 = jnp.float32
MESH = pl.DeviceIdType.MESH
EPS = 1e-05

SEQS = 6
ROWS = 128
HALF = 64
RES = 1024
WIDTH = 256
HEADS = 8
HD = 32
PEERS = 8
CH = 2
NCH = HEADS // CH
COEF = 16

NN = (((1,), (0,)), ((), ()))
NT = (((1,), (1,)), ((), ()))
TT = (((0,), (1,)), ((), ()))


def dot(a, b, dims=NN):
    return lax.dot_general(a, b, dims, preferred_element_type=F32)


def layer_norm_parts(x):
    mean = jnp.mean(x, -1, keepdims=True)
    cen = x - mean
    var = jnp.mean(cen * cen, -1, keepdims=True)
    rstd = lax.rsqrt(var + EPS)
    return cen * rstd, rstd


def split(x):
    hi = x.astype(BF)
    return hi, (x - hi.astype(F32)).astype(BF)


def main_kernel(
    x_ref, pair_ref, g_ref, wq, wk, wv, wg, wo, wpt_ref, mask_ref, keep_ref,
    out_ref, coef_ref,
    xraw, graw, xg, bias, dbias, btmp, stat, kt, vt, q_s, do_s, doT, qT, o_s, dq_s, dkt, dvt,
    dg_s, gt_s, dnear, dfar, rsbuf, ostage, orecv, dxs, dxr, dbs, dbr,
    sx_s, sx_r, ag_s, ag_r, rs_s, rs_r, bi_s, bi_r, bf_s, bf_r, dx_s, dx_r, ds_s, ds_r, oo_s, oo_r,
):
    sq = lax.axis_index("seq")
    rs = lax.axis_index("res")
    p = lax.rem(rs, 2)
    other = 1 - p
    y = lax.rem(lax.div(rs, 2), 4)
    xhi = lax.div(rs, 8)
    z = lax.rem(sq, 4)
    xlo = lax.div(sq, 4)
    partner = (sq, rs + 1 - 2 * p)
    x_peer = (sq, (1 - xhi) * 8 + y * 2 + p)
    lo_peer = ((1 - xlo) * 4 + z, rs)

    def ring(at, step):
        return lax.rem(at + step, 4)

    def y_peer(e):
        return (sq, xhi * 8 + ring(y, e) * 2 + p)

    def z_peer(e):
        return (xlo * 4 + ring(z, e), rs)

    def res_peer(i):
        hi = xhi if i < 4 else 1 - xhi
        return (sq, hi * 8 + ring(y, i % 4) * 2 + p)

    def seq_peer(i):
        hi = xlo if i < 4 else 1 - xlo
        return (hi * 4 + ring(z, i % 4), rs)

    def block(hi, at):
        return pl.ds(pl.multiple_of((hi * 4 + at) * ROWS, ROWS), ROWS)

    bar = pltpu.get_barrier_semaphore()
    for dev in [partner] + [f(i) for i in range(1, PEERS) for f in (res_peer, seq_peer)]:
        pl.semaphore_signal(bar, inc=1, device_id=dev, device_id_type=MESH)

    my_rows = pl.ds(pl.multiple_of(p * HALF, HALF), HALF)
    other_rows = pl.ds(pl.multiple_of(other * HALF, HALF), HALF)
    chip_rows = block(xhi, y)
    my_cols = block(xlo, z)

    def send(src, dst, s_sem, r_sem, dev):
        return pltpu.make_async_remote_copy(
            src_ref=src, dst_ref=dst, send_sem=s_sem, recv_sem=r_sem,
            device_id=dev, device_id_type=MESH,
        )

    def swap_copy(i, src, dst):
        return send(
            src.at[pl.ds(other * SEQS, SEQS)], dst.at[:, my_rows, :], sx_s.at[i], sx_r.at[i], partner
        )

    def gather_copy(s, e):
        blk = xg.at[s, chip_rows, :]
        return send(blk, blk, ag_s.at[s, e], ag_r.at[s, e], x_peer if e == 4 else y_peer(e))

    def gather_on(s, e, along_y):
        if along_y:
            blk, dev = xg.at[s, block(1 - xhi, y), :], y_peer(e)
        else:
            blk, dev = xg.at[s, block(xhi, ring(y, 4 - e)), :], x_peer
        return send(blk, blk, ag_s.at[s, 4 + e], ag_r.at[s, 4 + e], dev)

    def gather_first(s):
        for e in (4, 1, 2, 3):
            gather_copy(s, e).start()

    def gather_second(s):
        @pl.when(lax.rem(s, 2) == 0)
        def _():
            gather_copy(s, 4).wait_recv()
            for e in (1, 2, 3):
                gather_on(s, e, True).start()

        @pl.when(lax.rem(s, 2) == 1)
        def _():
            for e in (1, 2, 3):
                gather_copy(s, e).wait_recv()
                gather_on(s, e, False).start()

    def gather_rest(s):
        @pl.when(lax.rem(s, 2) == 0)
        def _():
            for e in (1, 2, 3):
                gather_copy(s, e).wait_recv()

        @pl.when(lax.rem(s, 2) == 1)
        def _():
            gather_copy(s, 4).wait_recv()

        for e in (1, 2, 3):
            gather_on(s, e, True).wait_recv()

    w_hi, w_lo = split(wpt_ref[...])
    left = jnp.concatenate(
        [jnp.concatenate([w_hi, w_hi], 1), jnp.concatenate([w_lo, jnp.zeros_like(w_lo)], 1)], 0
    )
    ones = jnp.ones((8, WIDTH), BF)
    square = jnp.full((128, 128), 1.0 / 128, BF)
    top_row = lax.broadcasted_iota(jnp.int32, (8, 128), 0) == 0

    def pair_body(i, carry):
        xb = pair_ref[i]
        cen = xb.astype(F32) - dot(xb, square)
        c_hi, c_lo = split(cen)
        s_hi, s_lo = split(cen * cen)
        proj = dot(left, jnp.concatenate([c_hi, c_lo], 1), NT)
        var = dot(ones, jnp.concatenate([s_hi, s_lo], 1), NT) * (1.0 / 128)
        mean = dot(ones[:, :128], xb, NT) * (1.0 / 128)
        rstd = lax.rsqrt(var + EPS)
        at = pl.ds(pl.multiple_of(i * 8, 8), 8)
        btmp[at, :] = (proj[0:8] + proj[8:16]) * rstd
        stat[at, :] = jnp.where(top_row, mean, rstd)
        return carry

    lax.fori_loop(0, HALF // 2, pair_body, 0, unroll=8)
    pl.semaphore_wait(bar, 2 * PEERS - 1)
    swaps = [swap_copy(0, x_ref, xraw), swap_copy(1, g_ref, graw)]
    for cp in swaps:
        cp.start()
    xraw[:, my_rows, :] = x_ref[pl.ds(p * SEQS, SEQS)]
    graw[:, my_rows, :] = g_ref[pl.ds(p * SEQS, SEQS)]

    lax.fori_loop(HALF // 2, HALF, pair_body, 0, unroll=8)

    def bias_copy(k, e):
        blk = bias.at[pl.ds(k * CH, CH), my_rows, my_cols]
        return send(blk, blk, bi_s.at[k, e], bi_r.at[k, e], lo_peer if e == 4 else z_peer(e))

    def bias_on(k, e):
        if k % 2 == 0:
            cols, dev = block(1 - xlo, z), z_peer(e)
        else:
            cols, dev = block(xlo, ring(z, 4 - e)), lo_peer
        blk = bias.at[pl.ds(k * CH, CH), my_rows, cols]
        return send(blk, blk, bi_s.at[k, 4 + e], bi_r.at[k, 4 + e], dev)

    def forward_copy(k):
        blk = bias.at[pl.ds(k * CH, CH), my_rows, :]
        return send(blk, blk, bf_s.at[k], bf_r.at[k], partner)

    usable = mask_ref[pl.ds(sq, 1), :] > 0
    for k in range(NCH):
        for h in range(k * CH, k * CH + CH):
            bias[h, my_rows, my_cols] = jnp.where(
                usable, btmp[pl.ds(h, HALF, stride=8), :], -1000000000.0
            )
        bias_copy(k, 4).start()

    def bias_first(k):
        for e in (1, 2, 3):
            bias_copy(k, e).start()

    bias_first(0)
    bias_first(1)

    def bias_second(k):
        if k % 2 == 0:
            bias_copy(k, 4).wait_recv()
            for e in (1, 2, 3):
                bias_on(k, e).start()
        else:
            for e in (1, 2, 3):
                bias_copy(k, e).wait_recv()
                bias_on(k, e).start()

    def bias_arrive(k):
        if k % 2 == 0:
            for e in (1, 2, 3):
                bias_copy(k, e).wait_recv()
        else:
            bias_copy(k, 4).wait_recv()
        for e in (1, 2, 3):
            bias_on(k, e).wait_recv()
        forward_copy(k).start()

    def norm(s):
        xhat, rstd = layer_norm_parts(xraw[s].astype(F32))
        xg[s, chip_rows, :] = xhat.astype(BF)

    def norm_body(s, carry):
        norm(s)
        return carry

    swaps[0].wait_recv()
    for s in (0, 1):
        norm(s)
        gather_first(s)
    lax.fori_loop(2, SEQS, norm_body, 0)
    bias_second(0)
    bias_first(2)
    gather_second(0)
    gather_first(2)
    gather_second(1)
    bias_second(1)
    bias_first(3)
    gather_first(3)
    bias_second(2)
    swaps[1].wait_recv()

    def scatter_y(s, e, hi):
        row = xhi if hi == 0 else 1 - xhi
        i = e + 3 * hi
        return send(
            dfar.at[s, :, block(row, ring(y, e))], rsbuf.at[s, i], rs_s.at[s, i], rs_r.at[s, i], y_peer(e)
        )

    def scatter_x_on(s):
        return send(
            dfar.at[s, :, block(1 - xhi, y)], rsbuf.at[s, 7], rs_s.at[s, 7], rs_r.at[s, 7], x_peer
        )

    def scatter_x(s, e):
        return send(
            dfar.at[s, :, block(1 - xhi, ring(y, e))], rsbuf.at[s, e], rs_s.at[s, e], rs_r.at[s, e], x_peer
        )

    def scatter_y_on(s, e):
        return send(
            dfar.at[s, :, block(xhi, ring(y, e))], rsbuf.at[s, 4 + e], rs_s.at[s, 4 + e], rs_r.at[s, 4 + e],
            y_peer(e),
        )

    def scatter_one(s, i):
        hi = xhi if i < 4 else 1 - xhi
        return send(
            dfar.at[s, :, block(hi, ring(y, i % 4))], rsbuf.at[s, i], rs_s.at[s, i], rs_r.at[s, i], res_peer(i)
        )

    def total(first, parts):
        out = first.astype(F32)
        for part in parts:
            out = out + part.astype(F32)
        return out

    def scatter_first(s):
        @pl.when(lax.rem(s, 2) == 0)
        def _():
            for e in (1, 2, 3):
                scatter_y(s, e, 1).start()
            for e in (1, 2, 3):
                scatter_y(s, e, 0).start()

        @pl.when(lax.rem(s, 2) == 1)
        def _():
            for e in (1, 2, 3, 0):
                scatter_x(s, e).start()

    def scatter_second(s):
        @pl.when(lax.rem(s, 2) == 0)
        def _():
            for e in (1, 2, 3):
                scatter_y(s, e, 1).wait_recv()
            blk = block(1 - xhi, y)
            dfar[s, :, blk] = total(dfar[s, :, blk], [rsbuf[s, 3 + e] for e in (1, 2, 3)]).astype(BF)
            scatter_x_on(s).start()

        @pl.when(lax.rem(s, 2) == 1)
        def _():
            for e in (1, 2, 3):
                scatter_x(s, e).wait_recv()
                blk = block(xhi, ring(y, e))
                dfar[s, :, blk] = total(dfar[s, :, blk], [rsbuf[s, e]]).astype(BF)
                scatter_y_on(s, e).start()

    def scatter_last(s):
        @pl.when(lax.rem(s, 2) == 0)
        def _():
            for e in (1, 2, 3):
                scatter_y(s, e, 0).wait_recv()
            scatter_x_on(s).wait_recv()
            finish_seq(s, total(dfar[s, :, chip_rows], [rsbuf[s, e] for e in (1, 2, 3, 7)]))

        @pl.when(lax.rem(s, 2) == 1)
        def _():
            scatter_x(s, 0).wait_recv()
            for e in (1, 2, 3):
                scatter_y_on(s, e).wait_recv()
            finish_seq(s, total(dfar[s, :, chip_rows], [rsbuf[s, e] for e in (0, 4 + 1, 4 + 2, 4 + 3)]))

    def finish_seq(s, far):
        dn = dnear[s] + far.T
        xhat, rstd = layer_norm_parts(xraw[s].astype(F32))
        dx = rstd * (
            dn
            - jnp.mean(dn, -1, keepdims=True)
            - xhat * jnp.mean(dn * xhat, -1, keepdims=True)
        )
        ostage[s] = dx.astype(BF)

    def pair_swap(k):
        blk = pl.ds(k * CH, CH)
        return send(dxs.at[blk], dxr.at[blk], dx_s.at[k], dx_r.at[k], partner)

    def tile_copy(k, i):
        blk = pl.ds(k * CH, CH)
        hi = xlo if i < 4 else 1 - xlo
        return send(
            dbs.at[blk, :, block(hi, ring(z, i % 4))], dbr.at[i, blk], ds_s.at[k, i], ds_r.at[k, i], seq_peer(i)
        )

    def tiles_start(k):
        blk = pl.ds(k * CH, CH)
        dxs[blk] = dbias[blk, other_rows, :].astype(BF)
        pair_swap(k).start()

    def tiles_first(k):
        blk = pl.ds(k * CH, CH)
        pair_swap(k).wait_recv()
        dbs[blk] = (dbias[blk, my_rows, :] + dxr[blk].astype(F32)).astype(BF)
        for i in range(1, PEERS):
            tile_copy(k, i).start()

    def tiles_last(k):
        blk = pl.ds(k * CH, CH)
        for i in range(1, PEERS):
            tile_copy(k, i).wait_recv()
        return total(dbs[blk, :, my_cols], [dbr[i, blk] for i in range(1, PEERS)])

    scale = HD ** (-0.5)

    def prepare(s, t):
        gather_rest(s)
        x = xg[s]
        kt[t] = dot(wk[...], x, TT).astype(BF)
        vt[t] = dot(wv[...], x, TT).astype(BF)
        xq = xg[s, chip_rows, :]
        qf = dot(xq, wq[...]) * scale
        q_s[t] = qf.astype(BF)
        qT[t] = qf.T.astype(BF)
        gate = jax.nn.sigmoid(dot(xq, wg[...]))
        gt_s[t] = gate
        keep = keep_ref[p * SEQS + s].astype(F32)
        grad_in = (graw[s].astype(F32) * keep).astype(BF)
        dg = dot(grad_in, wo[...], NT)
        dg_s[t] = dg
        d_att = dg * gate
        do_s[t] = d_att.astype(BF)
        doT[t] = d_att.T.astype(BF)

    def scores(h, t):
        hs = slice(HD * h, HD * h + HD)
        logits = dot(q_s[t, :, hs], kt[t, hs, :]) + bias[h]
        return logits, dot(do_s[t, :, hs], vt[t, hs, :])

    def head(h, t, logits, d_prob, first):
        hs = slice(HD * h, HD * h + HD)
        top = jnp.max(logits, -1, keepdims=True)
        e = jnp.exp(logits - top)
        prob = e * (1.0 / jnp.sum(e, -1, keepdims=True))
        prob_half = prob.astype(BF)
        o_s[t, :, hs] = dot(prob_half, vt[t, hs, :], NT)
        d_log = prob * (d_prob - jnp.sum(prob * d_prob, -1, keepdims=True))
        if first:
            dbias[h] = d_log
        else:
            dbias[h] += d_log
        dlog_half = d_log.astype(BF)
        dq_s[t, :, hs] = (dot(dlog_half, kt[t, hs, :], NT) * scale).astype(BF)
        dkt[t, hs, :] = dot(qT[t, hs, :], dlog_half).astype(BF)
        dvt[t, hs, :] = dot(doT[t, hs, :], prob_half).astype(BF)

    def attention(items, first=None, hook=lambda n: None):
        held = scores(*items[0])
        for n, item in enumerate(items):
            ahead = scores(*items[n + 1]) if n + 1 < len(items) else None
            head(*item, *held, item[1] == first)
            hook(n)
            held = ahead

    def heads_of(t, *chunks):
        return [(h, t) for k in chunks for h in range(k * CH, k * CH + CH)]

    def finish(s, t):
        gate = gt_s[t]
        d_gate = (dg_s[t] * o_s[t] * gate * (1.0 - gate)).astype(BF)
        dfar[s] = (dot(wk[...], dkt[t]) + dot(wv[...], dvt[t])).astype(BF)
        return d_gate

    def near(s, t, d_gate):
        dnear[s] = dot(dq_s[t], wq[...], NT) + dot(d_gate, wg[...], NT)

    bias_arrive(0)
    prepare(0, 0)
    forward_copy(0).wait_recv()
    attention(heads_of(0, 0), 0)
    bias_second(3)
    bias_arrive(1)
    prepare(1, 1)
    forward_copy(1).wait_recv()
    gather_second(2)
    gather_first(4)
    attention(heads_of(0, 1) + heads_of(1, 0), 0)
    bias_arrive(2)
    gather_second(3)
    gather_first(5)
    attention(heads_of(1, 1), 0)
    forward_copy(2).wait_recv()
    gather_second(4)
    attention(heads_of(0, 2), 0)
    bias_arrive(3)
    attention(heads_of(1, 2), 0)
    forward_copy(3).wait_recv()
    gather_second(5)
    attention(heads_of(0, 3) + heads_of(1, 3), 0)
    for s in (0, 1):
        g0 = finish(s, s)
        scatter_first(s)
        near(s, s, g0)

    def seq_body(s, carry):
        prepare(s, 0)
        attention(heads_of(0, 0, 1, 2, 3))
        g0 = finish(s, 0)
        scatter_first(s)
        near(s, 0, g0)

        @pl.when(s == 2)
        def _():
            scatter_second(0)

        scatter_second(s - 1)

        @pl.when(s == 3)
        def _():
            scatter_last(0)

        @pl.when(s >= 3)
        def _():
            scatter_last(s - 2)

        return carry

    lax.fori_loop(2, SEQS - 1, seq_body, 0)

    last = SEQS - 1
    prepare(last, 1)

    def sending(n):
        if n % CH == CH - 1:
            k = n // CH
            tiles_start(k)
            if k > 0:
                tiles_first(k - 1)

    attention(heads_of(1, 0, 1, 2, 3), hook=sending)
    g0 = finish(last, 1)
    for i in (6, 5, 7, 2, 4, 1, 3):
        scatter_one(last, i).start()
    tiles_first(NCH - 1)
    near(last, 1, g0)
    scatter_second(last - 1)
    scatter_last(last - 2)

    def back_copy(i, at, n):
        return send(
            ostage.at[pl.ds(at, n), other_rows, :], orecv.at[pl.ds(at, n)], oo_s.at[i], oo_r.at[i], partner
        )

    backs = [back_copy(0, 0, last), back_copy(1, last, 1)]

    mean = stat[pl.ds(0, HALF, stride=8), :]
    rstd = stat[pl.ds(1, HALF, stride=8), :]
    coef_ref[...] = jnp.zeros_like(coef_ref)
    along = jnp.zeros((HALF, ROWS), F32)
    for k in range(NCH):
        tile = tiles_last(k)
        for i in range(CH):
            h = k * CH + i
            along = along + tile[i] * btmp[pl.ds(h, HALF, stride=8), :]
            coef_ref[pl.ds(h, HALF, stride=COEF), :] = tile[i] * rstd
        if k == 0:
            scatter_last(last - 1)
            backs[0].start()
    u = rstd * rstd * along * (1.0 / 128)
    coef_ref[pl.ds(HEADS, HALF, stride=COEF), :] = mean * u
    coef_ref[pl.ds(HEADS + 1, HALF, stride=COEF), :] = u

    for i in range(1, PEERS):
        scatter_one(last, i).wait_recv()
    finish_seq(last, total(dfar[last, :, chip_rows], [rsbuf[last, i] for i in range(1, PEERS)]))
    backs[1].start()
    out_ref[pl.ds(p * SEQS, SEQS)] = ostage[:, my_rows, :]
    for cp in backs:
        cp.wait_recv()
    out_ref[pl.ds(other * SEQS, SEQS)] = orecv[...]

    for cp in swaps:
        cp.wait_send()
    for cp in backs:
        cp.wait_send()
    for i in range(1, PEERS):
        scatter_one(last, i).wait_send()

    def drain_seq(s, carry):
        for e in (1, 2, 3, 4):
            gather_copy(s, e).wait_send()
        for e in (1, 2, 3):
            gather_on(s, e, True).wait_send()

        @pl.when(lax.rem(s, 2) == 0)
        def _():
            for e in (1, 2, 3):
                scatter_y(s, e, 0).wait_send()
                scatter_y(s, e, 1).wait_send()
            scatter_x_on(s).wait_send()

        @pl.when((lax.rem(s, 2) == 1) & (s < last))
        def _():
            for e in (0, 1, 2, 3):
                scatter_x(s, e).wait_send()
            for e in (1, 2, 3):
                scatter_y_on(s, e).wait_send()

        return carry

    lax.fori_loop(0, SEQS, drain_seq, 0)

    for k in range(NCH):
        forward_copy(k).wait_send()
        pair_swap(k).wait_send()
        for e in (1, 2, 3, 4):
            bias_copy(k, e).wait_send()
        for e in (1, 2, 3):
            bias_on(k, e).wait_send()
        for i in range(1, PEERS):
            tile_copy(k, i).wait_send()


def run_main(x, pair, g, wq, wk, wv, wg, wo, wpt, mask, keep):
    def vm(*shape, dt=BF):
        return pltpu.VMEM(shape, dt)

    dma = pltpu.SemaphoreType.DMA
    vmem = pl.BlockSpec(memory_space=pltpu.VMEM)
    smem = pl.BlockSpec(memory_space=pltpu.SMEM)
    return pl.pallas_call(
        main_kernel,
        out_shape=(
            jax.ShapeDtypeStruct(x.shape, BF),
            jax.ShapeDtypeStruct((HALF * COEF, ROWS), F32),
        ),
        in_specs=[vmem] * 10 + [smem],
        out_specs=[vmem, vmem],
        scratch_shapes=[
            vm(SEQS, ROWS, WIDTH),
            vm(SEQS, ROWS, WIDTH),
            vm(SEQS, RES, WIDTH),
            vm(HEADS, ROWS, RES, dt=F32),
            vm(HEADS, ROWS, RES, dt=F32),
            vm(HALF * 8, ROWS, dt=F32),
            vm(HALF * 8, ROWS, dt=F32),
            vm(2, WIDTH, RES),
            vm(2, WIDTH, RES),
            vm(2, ROWS, WIDTH),
            vm(2, ROWS, WIDTH),
            vm(2, WIDTH, ROWS),
            vm(2, WIDTH, ROWS),
            vm(2, ROWS, WIDTH, dt=F32),
            vm(2, ROWS, WIDTH),
            vm(2, WIDTH, RES),
            vm(2, WIDTH, RES),
            vm(2, ROWS, WIDTH, dt=F32),
            vm(2, ROWS, WIDTH, dt=F32),
            vm(SEQS, ROWS, WIDTH, dt=F32),
            vm(SEQS, WIDTH, RES),
            vm(SEQS, PEERS, WIDTH, ROWS),
            vm(SEQS, ROWS, WIDTH),
            vm(SEQS, HALF, WIDTH),
            vm(HEADS, HALF, RES),
            vm(HEADS, HALF, RES),
            vm(HEADS, HALF, RES),
            vm(PEERS, HEADS, HALF, ROWS),
            dma((2,)), dma((2,)),
            dma((SEQS, PEERS)), dma((SEQS, PEERS)),
            dma((SEQS, PEERS)), dma((SEQS, PEERS)),
            dma((NCH, PEERS)), dma((NCH, PEERS)),
            dma((NCH,)), dma((NCH,)),
            dma((NCH,)), dma((NCH,)),
            dma((NCH, PEERS)), dma((NCH, PEERS)),
            dma((2,)), dma((2,)),
        ],
        compiler_params=pltpu.CompilerParams(
            collective_id=0, has_side_effects=True, vmem_limit_bytes=56 * 2**20
        ),
        name="attention_backward",
    )(x, pair, g, wq, wk, wv, wg, wo, wpt, mask, keep)


PB = 16


def pair_kernel(pair_ref, coef_ref, wpt_ref, out_ref):
    w = wpt_ref[...]
    w_hi, w_lo = split(w - jnp.mean(w, -1, keepdims=True))
    one = jnp.ones((1, 128), BF)

    def rows(n):
        return jnp.zeros((n, 128), BF)

    first = jnp.concatenate(
        [jnp.concatenate([w_hi, one, rows(7)], 0), jnp.concatenate([rows(9), one, rows(6)], 0)], 1
    )
    second = jnp.concatenate([jnp.concatenate([w_lo, rows(8)], 0), rows(16)], 1)
    right = jnp.concatenate([first, first, first, second], 0)
    for i in range(PB):
        cf = coef_ref[i * COEF : (i + 1) * COEF, :]
        hi = cf.astype(BF)
        rest = cf - hi.astype(F32)
        mid, low = split(rest)
        both = lax.dot_general(
            jnp.concatenate([hi, mid, low, hi], 0), right, (((0,), (0,)), ((), ())),
            preferred_element_type=F32,
        )
        out_ref[i] = both[:, :128] - pair_ref[i].astype(F32) * both[:, 128:]


def run_pair(pair, coef, wpt):
    n = pair.shape[0]
    return pl.pallas_call(
        pair_kernel,
        grid=(n // PB,),
        out_shape=jax.ShapeDtypeStruct(pair.shape, F32),
        in_specs=[
            pl.BlockSpec((PB, 128, 128), lambda i: (i, 0, 0)),
            pl.BlockSpec((PB * COEF, 128), lambda i: (i, 0)),
            pl.BlockSpec((HEADS, 128), lambda i: (0, 0)),
        ],
        out_specs=pl.BlockSpec((PB, 128, 128), lambda i: (i, 0, 0)),
        name="pair_gradient",
    )(pair, coef, wpt)


def body(x, pair, g, wq, wk, wv, wg, wo, wp, mask, keep):
    wpt = wp.T
    dx, coef = run_main(x, pair, g, wq, wk, wv, wg, wo, wpt, mask.reshape(8, 128), keep)
    return dx, run_pair(pair, coef, wpt)


def solution(mesh):
    return jax.shard_map(
        body,
        mesh=mesh,
        in_specs=(
            P("seq", "res", None),
            P("res", "seq", None),
            P("seq", "res", None),
            P(),
            P(),
            P(),
            P(),
            P(),
            P(),
            P(),
            P("seq"),
        ),
        out_specs=(P("seq", "res", None), P("res", "seq", None)),
        check_vma=False,
    )
```

time: 164 us -> 116 us (0.71); the launches traced: 163 us -> 116 us
  Pallas kernels: 160 us -> 115 us
    pallas_call x1, Pallas kernels: 144 us -> 110 us  [run_main(): pl.pallas_call(main_kernel, out_shape=(jax.ShapeDtypeStruct(x.shape, BF),...]
    pallas_call x1, Pallas kernels: 15.9 us -> 5.22 us  [run_pair(): pl.pallas_call(pair_kernel, grid=(n // PB,), out_shape=jax.ShapeDtypeStru...]
where the time goes in v2:
time: 116 us
  Pallas kernels  115 us (99%)
    pallas_call x1, Pallas kernels, run_main(): pl.pallas_call(main_kernel, out_shape=(jax.ShapeDtypeStruct(x.shape, BF),...  110 us
    pallas_call x1, Pallas kernels, run_pair(): pl.pallas_call(pair_kernel, grid=(n // PB,), out_shape=jax.ShapeDtypeStru...  5.22 us

profile of v2, /device:TPU:1, one launch (start us, length us, event | category | flops | bytes accessed | tf_op | source)
XLA Modules:
  0.0 116.2 jit_solution(17633507754728714720)
XLA Ops:
  0.6 109.6 %attention_backward.1 = (bf16[12,64,256]{2,1,0:T(8,128)(2,1)}, f32[1024,128]{1,0:T(8,128)}) custom-call(bf16[12,64,256]{2,1,0:T(8,128)(2,1)} %x_ref.1, bf16[64,128,128]{2,1,0:T(8,128)(2,1)} %pair_ref.3, bf16[12,64,256]{2,1,0:T(8,128)(2,1)} %g_ref.1, bf16[256,256]{1,0:T(8,128)(2,1)} %wq.1, bf16[256,256]{1,0:T(8,128)(2,1)} %wk.1, bf16[256,256]{1,0:T(8,128)(2,1)} %wv.1, ...), custom_call_target="tpu_custom_call" | custom-call | tf_op jit(solution)/shard_map/attention_backward/pallas_call | solution.py:590
  110.2 0.0 copy-start
  110.2 5.2 %pair_gradient.1 = f32[64,128,128]{2,1,0:T(8,128)} custom-call(bf16[64,128,128]{2,1,0:T(8,128)(2,1)} %pair_ref.3, f32[1024,128]{1,0:T(8,128)} %get-tuple-element.5.coef_ref, f32[8,128]{1,0:T(8,128)} %bitcast.3), custom_call_target="tpu_custom_call" | custom-call | tf_op jit(solution)/shard_map/pair_gradient/pallas_call | solution.py:673
  115.4 0.0 copy-done
  115.4 0.7 copy.14
Async XLA Ops:
  110.2 5.2 %copy-start = (bf16[12,64,256]{2,1,0:T(8,128)(2,1)S(1)}, bf16[12,64,256]{2,1,0:T(8,128)(2,1)}, u32[]{:S(2)}) copy-start(bf16[12,64,256]{2,1,0:T(8,128)(2,1)} %get-tuple-element.8) | copy-start | bytes 1179652

commit v3 on v2

--- a/solution.py
+++ b/solution.py
@@ -114,40 +114,47 @@
             blk, dev = xg.at[s, block(xhi, ring(y, 4 - e)), :], x_peer
         return send(blk, blk, ag_s.at[s, 4 + e], ag_r.at[s, 4 + e], dev)
 
+    def gather_one(s, i):
+        blk = xg.at[s, chip_rows, :]
+        return send(blk, blk, ag_s.at[s, i], ag_r.at[s, i], res_peer(i))
+
+    def y_first(s):
+        return (lax.rem(s, 2) == 1) & (s >= 3)
+
     def gather_first(s):
         for e in (4, 1, 2, 3):
             gather_copy(s, e).start()
 
     def gather_second(s):
-        @pl.when(lax.rem(s, 2) == 0)
+        @pl.when(jnp.logical_not(y_first(s)))
         def _():
             gather_copy(s, 4).wait_recv()
             for e in (1, 2, 3):
                 gather_on(s, e, True).start()
 
-        @pl.when(lax.rem(s, 2) == 1)
+        @pl.when(y_first(s))
         def _():
             for e in (1, 2, 3):
                 gather_copy(s, e).wait_recv()
                 gather_on(s, e, False).start()
 
     def gather_rest(s):
-        @pl.when(lax.rem(s, 2) == 0)
+        @pl.when(jnp.logical_not(y_first(s)))
         def _():
             for e in (1, 2, 3):
                 gather_copy(s, e).wait_recv()
 
-        @pl.when(lax.rem(s, 2) == 1)
+        @pl.when(y_first(s))
         def _():
             gather_copy(s, 4).wait_recv()
 
         for e in (1, 2, 3):
             gather_on(s, e, True).wait_recv()
 
-    w_hi, w_lo = split(wpt_ref[...])
-    left = jnp.concatenate(
-        [jnp.concatenate([w_hi, w_hi], 1), jnp.concatenate([w_lo, jnp.zeros_like(w_lo)], 1)], 0
-    )
+    w = wpt_ref[...]
+    w_hi, w_mid = split(w - jnp.mean(w, -1, keepdims=True))
+    w_low = (w - jnp.mean(w, -1, keepdims=True) - w_hi.astype(F32) - w_mid.astype(F32)).astype(BF)
+    left = jnp.concatenate([w_hi, w_mid, w_low, jnp.ones((8, 128), BF)], 0)
     ones = jnp.ones((8, WIDTH), BF)
     square = jnp.full((128, 128), 1.0 / 128, BF)
     top_row = lax.broadcasted_iota(jnp.int32, (8, 128), 0) == 0
@@ -155,14 +162,13 @@
     def pair_body(i, carry):
         xb = pair_ref[i]
         cen = xb.astype(F32) - dot(xb, square)
-        c_hi, c_lo = split(cen)
         s_hi, s_lo = split(cen * cen)
-        proj = dot(left, jnp.concatenate([c_hi, c_lo], 1), NT)
+        proj = dot(left, xb, NT)
         var = dot(ones, jnp.concatenate([s_hi, s_lo], 1), NT) * (1.0 / 128)
-        mean = dot(ones[:, :128], xb, NT) * (1.0 / 128)
+        mean = proj[24:32] * (1.0 / 128)
         rstd = lax.rsqrt(var + EPS)
         at = pl.ds(pl.multiple_of(i * 8, 8), 8)
-        btmp[at, :] = (proj[0:8] + proj[8:16]) * rstd
+        btmp[at, :] = (proj[0:8] + (proj[8:16] + proj[16:24])) * rstd
         stat[at, :] = jnp.where(top_row, mean, rstd)
         return carry
 
@@ -236,19 +242,15 @@
         return carry
 
     swaps[0].wait_recv()
-    for s in (0, 1):
-        norm(s)
-        gather_first(s)
+    norm(0)
+    for i in (1, 3, 4, 2, 5, 7, 6):
+        gather_one(0, i).start()
+    norm(1)
+    gather_first(1)
     lax.fori_loop(2, SEQS, norm_body, 0)
     bias_second(0)
     bias_first(2)
-    gather_second(0)
     gather_first(2)
-    gather_second(1)
-    bias_second(1)
-    bias_first(3)
-    gather_first(3)
-    bias_second(2)
     swaps[1].wait_recv()
 
     def scatter_y(s, e, hi):
@@ -373,7 +375,6 @@
     scale = HD ** (-0.5)
 
     def prepare(s, t):
-        gather_rest(s)
         x = xg[s]
         kt[t] = dot(wk[...], x, TT).astype(BF)
         vt[t] = dot(wv[...], x, TT).astype(BF)
@@ -433,20 +434,28 @@
     def near(s, t, d_gate):
         dnear[s] = dot(dq_s[t], wq[...], NT) + dot(d_gate, wg[...], NT)
 
+    for i in range(1, PEERS):
+        gather_one(0, i).wait_recv()
+    prepare(0, 0)
+    gather_second(1)
+    gather_first(3)
+    bias_second(1)
+    bias_first(3)
+    bias_second(2)
     bias_arrive(0)
-    prepare(0, 0)
     forward_copy(0).wait_recv()
     attention(heads_of(0, 0), 0)
+    gather_second(2)
+    gather_first(4)
     bias_second(3)
     bias_arrive(1)
+    gather_rest(1)
     prepare(1, 1)
     forward_copy(1).wait_recv()
-    gather_second(2)
-    gather_first(4)
+    gather_second(3)
+    gather_first(5)
     attention(heads_of(0, 1) + heads_of(1, 0), 0)
     bias_arrive(2)
-    gather_second(3)
-    gather_first(5)
     attention(heads_of(1, 1), 0)
     forward_copy(2).wait_recv()
     gather_second(4)
@@ -455,38 +464,52 @@
     attention(heads_of(1, 2), 0)
     forward_copy(3).wait_recv()
     gather_second(5)
-    attention(heads_of(0, 3) + heads_of(1, 3), 0)
-    for s in (0, 1):
-        g0 = finish(s, s)
-        scatter_first(s)
-        near(s, s, g0)
+    attention(heads_of(0, 3), 0)
+    g0 = finish(0, 0)
+    scatter_first(0)
+    near(0, 0, g0)
+    attention(heads_of(1, 3), 0)
+    g0 = finish(1, 1)
+    scatter_first(1)
+    near(1, 1, g0)
+
+    two = 4
+    direct = (6, 5, 7, 2, 4, 1, 3)
 
     def seq_body(s, carry):
+        gather_rest(s)
         prepare(s, 0)
         attention(heads_of(0, 0, 1, 2, 3))
         g0 = finish(s, 0)
-        scatter_first(s)
+
+        @pl.when(s < two)
+        def _():
+            scatter_first(s)
+
+        @pl.when(s >= two)
+        def _():
+            for i in direct:
+                scatter_one(s, i).start()
+
         near(s, 0, g0)
 
-        @pl.when(s == 2)
+        @pl.when(s == 3)
         def _():
             scatter_second(0)
-
-        scatter_second(s - 1)
-
-        @pl.when(s == 3)
-        def _():
+            scatter_second(1)
+
+        @pl.when(s == 4)
+        def _():
+            scatter_second(2)
             scatter_last(0)
-
-        @pl.when(s >= 3)
-        def _():
-            scatter_last(s - 2)
+            scatter_last(1)
 
         return carry
 
     lax.fori_loop(2, SEQS - 1, seq_body, 0)
 
     last = SEQS - 1
+    gather_rest(last)
     prepare(last, 1)
 
     def sending(n):
@@ -495,15 +518,22 @@
             tiles_start(k)
             if k > 0:
                 tiles_first(k - 1)
+            if k == 1:
+                scatter_second(3)
 
     attention(heads_of(1, 0, 1, 2, 3), hook=sending)
     g0 = finish(last, 1)
-    for i in (6, 5, 7, 2, 4, 1, 3):
+    for i in direct:
         scatter_one(last, i).start()
     tiles_first(NCH - 1)
     near(last, 1, g0)
-    scatter_second(last - 1)
-    scatter_last(last - 2)
+    scatter_last(2)
+    scatter_last(3)
+
+    def scatter_end(s):
+        for i in range(1, PEERS):
+            scatter_one(s, i).wait_recv()
+        finish_seq(s, total(dfar[s, :, chip_rows], [rsbuf[s, i] for i in range(1, PEERS)]))
 
     def back_copy(i, at, n):
         return send(
@@ -523,15 +553,13 @@
             along = along + tile[i] * btmp[pl.ds(h, HALF, stride=8), :]
             coef_ref[pl.ds(h, HALF, stride=COEF), :] = tile[i] * rstd
         if k == 0:
-            scatter_last(last - 1)
+            scatter_end(last - 1)
             backs[0].start()
     u = rstd * rstd * along * (1.0 / 128)
     coef_ref[pl.ds(HEADS, HALF, stride=COEF), :] = mean * u
     coef_ref[pl.ds(HEADS + 1, HALF, stride=COEF), :] = u
 
-    for i in range(1, PEERS):
-        scatter_one(last, i).wait_recv()
-    finish_seq(last, total(dfar[last, :, chip_rows], [rsbuf[last, i] for i in range(1, PEERS)]))
+    scatter_end(last)
     backs[1].start()
     out_ref[pl.ds(p * SEQS, SEQS)] = ostage[:, my_rows, :]
     for cp in backs:
@@ -543,22 +571,29 @@
     for cp in backs:
         cp.wait_send()
     for i in range(1, PEERS):
-        scatter_one(last, i).wait_send()
+        gather_one(0, i).wait_send()
 
     def drain_seq(s, carry):
-        for e in (1, 2, 3, 4):
-            gather_copy(s, e).wait_send()
-        for e in (1, 2, 3):
-            gather_on(s, e, True).wait_send()
-
-        @pl.when(lax.rem(s, 2) == 0)
+        @pl.when(s > 0)
+        def _():
+            for e in (1, 2, 3, 4):
+                gather_copy(s, e).wait_send()
+            for e in (1, 2, 3):
+                gather_on(s, e, True).wait_send()
+
+        @pl.when(s >= two)
+        def _():
+            for i in range(1, PEERS):
+                scatter_one(s, i).wait_send()
+
+        @pl.when((lax.rem(s, 2) == 0) & (s < two))
         def _():
             for e in (1, 2, 3):
                 scatter_y(s, e, 0).wait_send()
                 scatter_y(s, e, 1).wait_send()
             scatter_x_on(s).wait_send()
 
-        @pl.when((lax.rem(s, 2) == 1) & (s < last))
+        @pl.when((lax.rem(s, 2) == 1) & (s < two))
         def _():
             for e in (0, 1, 2, 3):
                 scatter_x(s, e).wait_send()

time: 116 us -> 107 us (0.922)
  Pallas kernels: 115 us -> 105 us
    pallas_call x1, Pallas kernels: 110 us -> 99.9 us  [run_main(): pl.pallas_call(main_kernel, out_shape=(jax.ShapeDtypeStruct(x.shape, BF),...]
where the time goes in v3:
time: 107 us; the launch traced here: 106 us
  Pallas kernels  105 us (98%)
    pallas_call x1, Pallas kernels, run_main(): pl.pallas_call(main_kernel, out_shape=(jax.ShapeDtypeStruct(x.shape, BF),...  99.9 us
    pallas_call x1, Pallas kernels, run_pair(): pl.pallas_call(pair_kernel, grid=(n // PB,), out_shape=jax.ShapeDtypeStru...  5.21 us

profile of v3, /device:TPU:1, one launch (start us, length us, event | category | flops | bytes accessed | tf_op | source)
XLA Modules:
  0.0 106.5 jit_solution(7085042687348635912)
XLA Ops:
  0.6 99.9 %attention_backward.1 = (bf16[12,64,256]{2,1,0:T(8,128)(2,1)}, f32[1024,128]{1,0:T(8,128)}) custom-call(bf16[12,64,256]{2,1,0:T(8,128)(2,1)} %x_ref.1, bf16[64,128,128]{2,1,0:T(8,128)(2,1)} %pair_ref.3, bf16[12,64,256]{2,1,0:T(8,128)(2,1)} %g_ref.1, bf16[256,256]{1,0:T(8,128)(2,1)} %wq.1, bf16[256,256]{1,0:T(8,128)(2,1)} %wk.1, bf16[256,256]{1,0:T(8,128)(2,1)} %wv.1, ...), custom_call_target="tpu_custom_call" | custom-call | tf_op jit(solution)/shard_map/attention_backward/pallas_call | solution.py:625
  100.5 0.0 copy-start
  100.5 5.2 %pair_gradient.1 = f32[64,128,128]{2,1,0:T(8,128)} custom-call(bf16[64,128,128]{2,1,0:T(8,128)(2,1)} %pair_ref.3, f32[1024,128]{1,0:T(8,128)} %get-tuple-element.5.coef_ref, f32[8,128]{1,0:T(8,128)} %bitcast.3), custom_call_target="tpu_custom_call" | custom-call | tf_op jit(solution)/shard_map/pair_gradient/pallas_call | solution.py:708
  105.7 0.0 copy-done
  105.7 0.7 copy.14
Async XLA Ops:
  100.5 5.2 %copy-start = (bf16[12,64,256]{2,1,0:T(8,128)(2,1)S(1)}, bf16[12,64,256]{2,1,0:T(8,128)(2,1)}, u32[]{:S(2)}) copy-start(bf16[12,64,256]{2,1,0:T(8,128)(2,1)} %get-tuple-element.8) | copy-start | bytes 1179652

commit v4 on v3

--- a/solution.py
+++ b/solution.py
@@ -187,7 +187,7 @@
         return send(blk, blk, bi_s.at[k, e], bi_r.at[k, e], lo_peer if e == 4 else z_peer(e))
 
     def bias_on(k, e):
-        if k % 2 == 0:
+        if k % 2 == 0 or k == 3:
             cols, dev = block(1 - xlo, z), z_peer(e)
         else:
             cols, dev = block(xlo, ring(z, 4 - e)), lo_peer
@@ -214,7 +214,7 @@
     bias_first(1)
 
     def bias_second(k):
-        if k % 2 == 0:
+        if k % 2 == 0 or k == 3:
             bias_copy(k, 4).wait_recv()
             for e in (1, 2, 3):
                 bias_on(k, e).start()
@@ -224,7 +224,7 @@
                 bias_on(k, e).start()
 
     def bias_arrive(k):
-        if k % 2 == 0:
+        if k % 2 == 0 or k == 3:
             for e in (1, 2, 3):
                 bias_copy(k, e).wait_recv()
         else:
@@ -354,6 +354,19 @@
             dbs.at[blk, :, block(hi, ring(z, i % 4))], dbr.at[i, blk], ds_s.at[k, i], ds_r.at[k, i], seq_peer(i)
         )
 
+    def tile_z(k, e, i):
+        blk = pl.ds(k * CH, CH)
+        hi = xlo if i < 4 else 1 - xlo
+        return send(
+            dbs.at[blk, :, block(hi, ring(z, e))], dbr.at[i, blk], ds_s.at[k, i], ds_r.at[k, i], z_peer(e)
+        )
+
+    def tile_lo(k):
+        blk = pl.ds(k * CH, CH)
+        return send(
+            dbs.at[blk, :, block(1 - xlo, z)], dbr.at[4, blk], ds_s.at[k, 4], ds_r.at[k, 4], lo_peer
+        )
+
     def tiles_start(k):
         blk = pl.ds(k * CH, CH)
         dxs[blk] = dbias[blk, other_rows, :].astype(BF)
@@ -363,14 +376,33 @@
         blk = pl.ds(k * CH, CH)
         pair_swap(k).wait_recv()
         dbs[blk] = (dbias[blk, my_rows, :] + dxr[blk].astype(F32)).astype(BF)
-        for i in range(1, PEERS):
-            tile_copy(k, i).start()
+        if k == NCH - 1:
+            for i in range(1, PEERS):
+                tile_copy(k, i).start()
+        else:
+            for e in (1, 2, 3):
+                tile_z(k, e, e + 4).start()
+            for e in (1, 2, 3):
+                tile_z(k, e, e).start()
+
+    def tiles_second(k):
+        blk = pl.ds(k * CH, CH)
+        for e in (1, 2, 3):
+            tile_z(k, e, e + 4).wait_recv()
+        cols = block(1 - xlo, z)
+        dbs[blk, :, cols] = total(dbs[blk, :, cols], [dbr[i, blk] for i in (5, 6, 7)]).astype(BF)
+        tile_lo(k).start()
 
     def tiles_last(k):
         blk = pl.ds(k * CH, CH)
-        for i in range(1, PEERS):
-            tile_copy(k, i).wait_recv()
-        return total(dbs[blk, :, my_cols], [dbr[i, blk] for i in range(1, PEERS)])
+        if k == NCH - 1:
+            for i in range(1, PEERS):
+                tile_copy(k, i).wait_recv()
+            return total(dbs[blk, :, my_cols], [dbr[i, blk] for i in range(1, PEERS)])
+        for e in (1, 2, 3):
+            tile_z(k, e, e).wait_recv()
+        tile_lo(k).wait_recv()
+        return total(dbs[blk, :, my_cols], [dbr[i, blk] for i in (1, 2, 3, 4)])
 
     scale = HD ** (-0.5)
 
@@ -518,8 +550,10 @@
             tiles_start(k)
             if k > 0:
                 tiles_first(k - 1)
-            if k == 1:
+            if k == 2:
                 scatter_second(3)
+            if k == 3:
+                tiles_second(0)
 
     attention(heads_of(1, 0, 1, 2, 3), hook=sending)
     g0 = finish(last, 1)
@@ -527,8 +561,10 @@
         scatter_one(last, i).start()
     tiles_first(NCH - 1)
     near(last, 1, g0)
+    tiles_second(1)
     scatter_last(2)
     scatter_last(3)
+    tiles_second(2)
 
     def scatter_end(s):
         for i in range(1, PEERS):
@@ -611,8 +647,14 @@
             bias_copy(k, e).wait_send()
         for e in (1, 2, 3):
             bias_on(k, e).wait_send()
-        for i in range(1, PEERS):
-            tile_copy(k, i).wait_send()
+        if k == NCH - 1:
+            for i in range(1, PEERS):
+                tile_copy(k, i).wait_send()
+        else:
+            for e in (1, 2, 3):
+                tile_z(k, e, e).wait_send()
+                tile_z(k, e, e + 4).wait_send()
+            tile_lo(k).wait_send()
 
 
 def run_main(x, pair, g, wq, wk, wv, wg, wo, wpt, mask, keep):

time: 107 us -> 104 us (0.972)
  Pallas kernels: 105 us -> 102 us
    pallas_call x1, Pallas kernels: 99.9 us -> 96.8 us  [run_main(): pl.pallas_call(main_kernel, out_shape=(jax.ShapeDtypeStruct(x.shape, BF),...]
where the time goes in v4:
time: 104 us; the launch traced here: 103 us
  Pallas kernels  102 us (98%)
    pallas_call x1, Pallas kernels, run_main(): pl.pallas_call(main_kernel, out_shape=(jax.ShapeDtypeStruct(x.shape, BF),...  96.8 us
    pallas_call x1, Pallas kernels, run_pair(): pl.pallas_call(pair_kernel, grid=(n // PB,), out_shape=jax.ShapeDtypeStru...  5.21 us

profile of v4, /device:TPU:1, one launch (start us, length us, event | category | flops | bytes accessed | tf_op | source)
XLA Modules:
  0.0 103.4 jit_solution(12173555064317395531)
XLA Ops:
  0.6 96.8 %attention_backward.1 = (bf16[12,64,256]{2,1,0:T(8,128)(2,1)}, f32[1024,128]{1,0:T(8,128)}) custom-call(bf16[12,64,256]{2,1,0:T(8,128)(2,1)} %x_ref.1, bf16[64,128,128]{2,1,0:T(8,128)(2,1)} %pair_ref.3, bf16[12,64,256]{2,1,0:T(8,128)(2,1)} %g_ref.1, bf16[256,256]{1,0:T(8,128)(2,1)} %wq.1, bf16[256,256]{1,0:T(8,128)(2,1)} %wk.1, bf16[256,256]{1,0:T(8,128)(2,1)} %wv.1, ...), custom_call_target="tpu_custom_call" | custom-call | tf_op jit(solution)/shard_map/attention_backward/pallas_call | solution.py:667
  97.4 0.0 copy-start
  97.4 5.2 %pair_gradient.1 = f32[64,128,128]{2,1,0:T(8,128)} custom-call(bf16[64,128,128]{2,1,0:T(8,128)(2,1)} %pair_ref.3, f32[1024,128]{1,0:T(8,128)} %get-tuple-element.5.coef_ref, f32[8,128]{1,0:T(8,128)} %bitcast.3), custom_call_target="tpu_custom_call" | custom-call | tf_op jit(solution)/shard_map/pair_gradient/pallas_call | solution.py:750
  102.6 0.0 copy-done
  102.6 0.7 copy.14
Async XLA Ops:
  97.4 5.2 %copy-start = (bf16[12,64,256]{2,1,0:T(8,128)(2,1)S(1)}, bf16[12,64,256]{2,1,0:T(8,128)(2,1)}, u32[]{:S(2)}) copy-start(bf16[12,64,256]{2,1,0:T(8,128)(2,1)} %get-tuple-element.8) | copy-start | bytes 1179652

commit v5 on v4

--- a/solution.py
+++ b/solution.py
@@ -668,7 +668,7 @@
         main_kernel,
         out_shape=(
             jax.ShapeDtypeStruct(x.shape, BF),
-            jax.ShapeDtypeStruct((HALF * COEF, ROWS), F32),
+            jax.ShapeDtypeStruct(((HALF + 1) * COEF, ROWS), F32),
         ),
         in_specs=[vmem] * 10 + [smem],
         out_specs=[vmem, vmem],
@@ -678,8 +678,8 @@
             vm(SEQS, RES, WIDTH),
             vm(HEADS, ROWS, RES, dt=F32),
             vm(HEADS, ROWS, RES, dt=F32),
-            vm(HALF * 8, ROWS, dt=F32),
-            vm(HALF * 8, ROWS, dt=F32),
+            vm(HALF * 8 + 8, ROWS, dt=F32),
+            vm(HALF * 8 + 8, ROWS, dt=F32),
             vm(2, WIDTH, RES),
             vm(2, WIDTH, RES),
             vm(2, ROWS, WIDTH),

time: 104 us -> 104 us (level)
  no operation moved by 1% of the time
where the time goes in v5:
time: 104 us; the launch traced here: 103 us
  Pallas kernels  102 us (98%)
    pallas_call x1, Pallas kernels, run_main(): pl.pallas_call(main_kernel, out_shape=(jax.ShapeDtypeStruct(x.shape, BF),...  96.8 us
    pallas_call x1, Pallas kernels, run_pair(): pl.pallas_call(pair_kernel, grid=(n // PB,), out_shape=jax.ShapeDtypeStru...  5.19 us

profile of v5, /device:TPU:1, one launch (start us, length us, event | category | flops | bytes accessed | tf_op | source)
XLA Modules:
  0.0 103.4 jit_solution(16399844058188473243)
XLA Ops:
  0.6 96.8 %attention_backward.1 = (bf16[12,64,256]{2,1,0:T(8,128)(2,1)}, f32[1040,128]{1,0:T(8,128)}) custom-call(bf16[12,64,256]{2,1,0:T(8,128)(2,1)} %x_ref.1, bf16[64,128,128]{2,1,0:T(8,128)(2,1)} %pair_ref.3, bf16[12,64,256]{2,1,0:T(8,128)(2,1)} %g_ref.1, bf16[256,256]{1,0:T(8,128)(2,1)} %wq.1, bf16[256,256]{1,0:T(8,128)(2,1)} %wk.1, bf16[256,256]{1,0:T(8,128)(2,1)} %wv.1, ...), custom_call_target="tpu_custom_call" | custom-call | tf_op jit(solution)/shard_map/attention_backward/pallas_call | solution.py:667
  97.4 0.0 copy-start
  97.5 5.2 %pair_gradient.1 = f32[64,128,128]{2,1,0:T(8,128)} custom-call(bf16[64,128,128]{2,1,0:T(8,128)(2,1)} %pair_ref.3, f32[1040,128]{1,0:T(8,128)} %get-tuple-element.5.coef_ref, f32[8,128]{1,0:T(8,128)} %bitcast.3), custom_call_target="tpu_custom_call" | custom-call | tf_op jit(solution)/shard_map/pair_gradient/pallas_call | solution.py:750
  102.6 0.0 copy-done
  102.6 0.7 copy.14
Async XLA Ops:
  97.4 5.2 %copy-start = (bf16[12,64,256]{2,1,0:T(8,128)(2,1)S(1)}, bf16[12,64,256]{2,1,0:T(8,128)(2,1)}, u32[]{:S(2)}) copy-start(bf16[12,64,256]{2,1,0:T(8,128)(2,1)} %get-tuple-element.8) | copy-start | bytes 1179652
